TPU v7x, 256 devices: a whole 4x4x8 slice. The times are simulated.
256 devices in a mesh: seq: 128 (over y_hi, z, x, core), ch: 2 (over y_lo).
Axes of the slice: x: 4, y: 4 (y_hi: 2, y_lo: 2; y = y_hi * 2 + y_lo), z: 8, core: 2. Of those that a mesh axis runs over, the one named last changes fastest.
Arguments:
- features: bfloat16 [131072, 4096], P('seq', 'ch'), may hold values from -6 to 6
- value_weight: bfloat16 [4096, 512], P('ch'), may hold values from -0.09375 to 0.09375
- gate_weight: bfloat16 [4096, 512], P('ch'), may hold values from -0.09375 to 0.09375
- kernel: bfloat16 [1024, 512], P('seq', 'ch'), may hold values from -0.5 to 0.5
- skip_gain: float32 [512], P('ch'), may hold values from 0.5 to 1.5
Outputs:
- mixed: bfloat16 [131072, 512], P('seq', 'ch')
All inputs are finite; a program needn't handle non-finite values.
Results may differ from a plain program's by a relative error of at most 0.0049.
Values may be sent and summed in bfloat16 or wider, within the bound.
A program may use at most 128 MiB of HBM per device.

v0:
```python
import math

import jax
import jax.numpy as jnp
from jax import lax
from jax.sharding import PartitionSpec as P


def from_behind(value, axis, steps):
    count = lax.axis_size(axis)
    leading, last = (max(0, -steps), min(count, count - steps))
    return lax.ppermute(value, axis, [(source, source + steps) for source in range(leading, last)])


def forward_tables(period, bin_count, row_count):
    freq = lax.broadcasted_iota(jnp.int32, (bin_count, row_count), 0)
    place = lax.broadcasted_iota(jnp.int32, (bin_count, row_count), 1)
    phase = (freq * place % period).astype(jnp.float32) * (2.0 * math.pi / period)
    return (jnp.cos(phase), jnp.sin(phase))


def inverse_tables(period, bin_count, first_row, row_count):
    place = lax.broadcasted_iota(jnp.int32, (row_count, bin_count), 0) + first_row
    freq = lax.broadcasted_iota(jnp.int32, (row_count, bin_count), 1)
    phase = (freq * place % period).astype(jnp.float32) * (2.0 * math.pi / period)
    half = period // 2
    weight = jnp.where((freq == 0) | (freq == half), 1.0, 2.0)
    weight = jnp.where(freq <= half, weight, 0.0) / period
    return (jnp.cos(phase) * weight, jnp.sin(phase) * weight)


def spectral_conv(kernel_full, source, period, first_out, out_rows):
    bin_count = (period // 2 + 1 + 127) // 128 * 128
    cos_fwd, sin_fwd = forward_tables(period, bin_count, source.shape[0])
    exact = lax.Precision.HIGHEST
    values = source.astype(jnp.float32)
    taps = kernel_full.astype(jnp.float32)
    tap_count = taps.shape[0]
    val_cos = jnp.dot(cos_fwd, values, precision=exact, preferred_element_type=jnp.float32)
    val_sin = jnp.dot(sin_fwd, values, precision=exact, preferred_element_type=jnp.float32)
    ker_cos = jnp.dot(
        cos_fwd[:, :tap_count], taps, precision=exact, preferred_element_type=jnp.float32
    )
    ker_sin = jnp.dot(
        sin_fwd[:, :tap_count], taps, precision=exact, preferred_element_type=jnp.float32
    )
    prod_cos = val_cos * ker_cos - val_sin * ker_sin
    prod_sin = val_sin * ker_cos + val_cos * ker_sin
    cos_inv, sin_inv = inverse_tables(period, bin_count, first_out, out_rows)
    return jnp.dot(
        cos_inv, prod_cos, precision=exact, preferred_element_type=jnp.float32
    ) + jnp.dot(sin_inv, prod_sin, precision=exact, preferred_element_type=jnp.float32)


def on_device(features, value_weight, gate_weight, kernel, skip_gain):
    value_partial = jnp.dot(features, value_weight, preferred_element_type=jnp.float32)
    gate_partial = jnp.dot(features, gate_weight, preferred_element_type=jnp.float32)
    value_summed, gate_sum = (
        lax.psum_scatter(value_partial, "ch", scatter_dimension=1, tiled=True),
        lax.psum_scatter(gate_partial, "ch", scatter_dimension=1, tiled=True),
    )
    projected = value_summed.astype(jnp.bfloat16)
    kernel_full = lax.all_gather(kernel, "seq", axis=0, tiled=True)
    row_count = projected.shape[0]
    preceding = from_behind(projected, "seq", 1)
    extended = jnp.concatenate([preceding, projected], 0)
    convolved = spectral_conv(kernel_full, extended, 2 * row_count, row_count, row_count)
    mixed = (convolved + skip_gain[None, :] * projected.astype(jnp.float32)) * jax.nn.silu(gate_sum)
    return mixed.astype(jnp.bfloat16)


def solution(mesh):
    return jax.shard_map(
        on_device,
        mesh=mesh,
        in_specs=(P("seq", "ch"), P("ch", None), P("ch", None), P("seq", "ch"), P("ch")),
        out_specs=P("seq", "ch"),
        check_vma=False,
    )
```

profile of v0, /device:TPU:24, one launch (start us, length us, event | category | flops | bytes accessed | tf_op | source)
XLA Modules:
  0.0 466.1 jit_solution(16916356706658735101)
XLA Ops:
  6.5 0.0 copy-start
  6.5 0.0 reduce-scatter.3.cloned.1.call-start
  6.5 1.6 copy-done
  8.1 5.9 %fusion.80 = f32[1024,512]{1,0:T(8,128)} fusion(bf16[1024,2048]{1,0:T(8,128)(2,1)} %param.5, bf16[2048,512]{1,0:T(8,128)(2,1)S(1)} %copy-done), kind=kOutput, calls=%fused_computation.80 | convolution fusion | flops 2147483648 | bytes 8388608 | tf_op jit(solution)/shard_map/dot_general | solution.py:56
  14.1 0.0 reduce-scatter.3.cloned.1.call-update
  14.1 0.0 reduce-scatter.5.cloned.1.call-start
  14.1 6.5 %fusion.81 = f32[1024,512]{1,0:T(8,128)} fusion(bf16[1024,2048]{1,0:T(8,128)(2,1)} %param.5, bf16[2048,512]{1,0:T(8,128)(2,1)} %param.7), kind=kOutput, calls=%fused_computation.81 | convolution fusion | flops 2147483648 | bytes 8388608 | tf_op jit(solution)/shard_map/dot_general | solution.py:57
  20.6 0.0 reduce-scatter.5.cloned.1.call-update
  20.7 34.1 %fusion.17 = f32[1152,2048]{1,0:T(8,128)S(1)} fusion(), kind=kLoop, calls=%fused_computation.23 | loop fusion | flops 33030144 | bytes 9437184 | tf_op jit(solution)/shard_map/cos | solution.py:19
  54.8 0.0 copy-start.3
  54.8 35.7 %fusion.16 = f32[1152,2048]{1,0:T(8,128)} fusion(), kind=kLoop, calls=%fused_computation.22 | loop fusion | flops 33030144 | bytes 9437184 | tf_op jit(solution)/shard_map/sin | solution.py:19
  90.5 0.0 copy-done.3
  90.5 184.9 %all_gather.3 = bf16[1024,256]{1,0:T(8,128)(2,1)S(1)} all-gather(bf16[8,256]{1,0:T(8,128)(2,1)S(1)} %copy-done.3), channel_id=1, replica_groups=mesh['seq'=128,'ch'=2] {'seq'}, dimensions={0}, use_global_device_ids=true | all-gather | bytes 528384 | tf_op jit(solution)/shard_map/all_gather | solution.py:63
  275.4 3.3 fusion.11
  278.7 1.3 convert_element_type.27
  280.0 2.3 collective-permute-start
  282.3 4.6 fusion.9
  286.9 0.0 copy-start.2
  286.9 9.3 %collective-permute-done = bf16[1024,256]{1,0:T(8,128)(2,1)S(1)} collective-permute-done((bf16[1024,256]{1,0:T(8,128)(2,1)S(1)}, bf16[1024,256]{1,0:T(8,128)(2,1)S(1)}, u32[]{:S(2)}, u32[]{:S(2)}) %collective-permute-start) | collective-permute-done | bytes 524320 | tf_op jit(solution)/shard_map/ppermute | solution.py:12
  296.2 0.1 pad_maximum_fusion.10
  296.3 0.1 pad_maximum_fusion.9
  296.3 56.0 %fusion.26 = f32[1152,256]{1,0:T(8,128)S(1)} fusion(bf16[2048,256]{1,0:T(8,128)(2,1)S(1)} %pad_maximum_fusion.10), kind=kOutput, calls=%fused_computation.32 | convolution fusion | flops 7280787456 | bytes 2228224 | tf_op jit(solution)/shard_map/dot_general | solution.py:40
  352.4 0.0 copy-start.5
  352.4 55.8 %fusion.24 = f32[1152,256]{1,0:T(8,128)S(1)} fusion(bf16[2048,256]{1,0:T(8,128)(2,1)S(1)} %pad_maximum_fusion.9), kind=kOutput, calls=%fused_computation.31 | convolution fusion | flops 7280787456 | bytes 2228224 | tf_op jit(solution)/shard_map/dot_general | solution.py:39
  408.2 0.0 copy-done.2
  408.2 0.0 copy-done.5
  408.2 0.0 copy-start.6
  408.2 1.0 copy-done.6
  409.3 0.0 copy-done.1
  409.3 23.7 %fusion.13 = f32[1024,256]{1,0:T(8,128)} fusion(f32[1152]{0:T(1024)S(1)} %fusion.57, s32[1024]{0:T(1024)S(1)} %iota_add_fusion, pred[1152]{0:T(1024)(128)(4,1)S(1)} %iota_compare_fusion.2, f32[1152,256]{1,0:T(8,128)S(1)} %fusion.24, f32[1152,256]{1,0:T(8,128)S(1)} %fusion.9, f32[1152,256]{1,0:T(8,128)S(1)} %fusion.26, f32[1152,256]{1,0:T(8,128)S(1)} %copy-done.1), kind=kOutput, calls=%fused_computation.19 | convolution fusion | flops 3644817408 | bytes 5777024 | tf_op jit(solution)/shard_map/dot_general | solution.py:52
  433.0 0.0 copy-done.4
  433.0 26.0 %fusion.47 = bf16[1024,256]{1,0:T(8,128)(2,1)} fusion(f32[1024,256]{1,0:T(8,128)} %fusion.13, f32[1152]{0:T(1024)S(1)} %fusion.57, s32[1024]{0:T(1024)S(1)} %iota_add_fusion, pred[1152]{0:T(1024)(128)(4,1)S(1)} %iota_compare_fusion.2, f32[1152,256]{1,0:T(8,128)} %copy-done.5, f32[1152,256]{1,0:T(8,128)} %copy-done.2, f32[1152,256]{1,0:T(8,128)} %copy-done.6, ...), kind=kOutput, calls=%fused_computation.44 | convolution fusion | flops 3647438848 | bytes 7875200 | tf_op jit(solution)/shard_map/dot_general | solution.py:50
  (7 shorter events, 0.0 us)
Async XLA Ops:
  6.5 1.6 copy-start
  6.5 272.2 %reduce-scatter.3.cloned.1.call-start = ((), (), s32[]{:S(2)}) async-start(), calls=%async_computation.2 | async-start | bytes 3145728 | tf_op jit(solution)/shard_map/reduce_scatter | solution.py:59
  14.1 418.9 %reduce-scatter.5.cloned.1.call-start = ((), (), s32[]{:S(2)}) async-start(), calls=%async_computation.3 | async-start | bytes 3145728 | tf_op jit(solution)/shard_map/reduce_scatter | solution.py:60
  54.8 35.7 %copy-start.3 = (bf16[8,256]{1,0:T(8,128)(2,1)S(1)}, bf16[8,256]{1,0:T(8,128)(2,1)}, u32[]{:S(2)}) copy-start(bf16[8,256]{1,0:T(8,128)(2,1)} %param.8) | copy-start | bytes 12292
  280.0 16.2 %collective-permute-start = (bf16[1024,256]{1,0:T(8,128)(2,1)S(1)}, bf16[1024,256]{1,0:T(8,128)(2,1)S(1)}, u32[]{:S(2)}, u32[]{:S(2)}) collective-permute-start(bf16[1024,256]{1,0:T(8,128)(2,1)S(1)} %convert_element_type.27), channel_id=1, source_target_pairs={{0,2},{2,4},{4,6},{6,8},{8,10},{10,12},{12,14},{14,16},{16,18},{18... | collective-permute-start | bytes 1572872 | tf_op jit(solution)/shard_map/ppermute | solution.py:12
  286.9 121.3 %copy-start.2 = (f32[1152,256]{1,0:T(8,128)}, f32[1152,256]{1,0:T(8,128)S(1)}, u32[]{:S(2)}) copy-start(f32[1152,256]{1,0:T(8,128)S(1)} %fusion.9) | copy-start | bytes 3538948
  352.4 55.8 %copy-start.5 = (f32[1152,256]{1,0:T(8,128)}, f32[1152,256]{1,0:T(8,128)S(1)}, u32[]{:S(2)}) copy-start(f32[1152,256]{1,0:T(8,128)S(1)} %fusion.26) | copy-start | bytes 3538948
  352.4 56.9 %copy-start.1 = (f32[1152,256]{1,0:T(8,128)S(1)}, f32[1152,256]{1,0:T(8,128)}, u32[]{:S(2)}) copy-start(f32[1152,256]{1,0:T(8,128)} %fusion.11) | copy-start | bytes 3538948
  408.2 1.0 copy-start.6
  409.3 23.7 %copy-start.4 = (f32[256]{0:T(256)S(1)}, f32[256]{0:T(256)}, u32[]{:S(2)}) copy-start(f32[256]{0:T(256)} %param.9) | copy-start | bytes 3076
Sparse Core Ops, SparseCore 0:
  14.2 38.9 reduce-scatter.2
  55.9 37.9 reduce-scatter.4
where the time goes:
time: 469 us; the launch traced here: 466 us
  blocking collectives  185 us (39%)
  matrix products  182 us (39%)
  other arithmetic  71.2 us (15%)
  between operations  13.7 us (3%)
  waiting for transfers between devices  9.32 us (2%)
    all_gather x1, blocking collectives, on_device(): kernel_full = lax.all_gather(kernel, 'seq', axis=0, tiled=True)  185 us
    dot_general x1, matrix products, spectral_conv(): jnp.dot(sin_fwd, values, precision=exact, preferred_element_type=jnp.floa...  56 us
    dot_general x1, matrix products, spectral_conv(): jnp.dot(cos_fwd, values, precision=exact, preferred_element_type=jnp.floa...  55.8 us
    sin x1, other arithmetic, forward_tables(): return (jnp.cos(phase), jnp.sin(phase))  35.7 us
    cos x1, other arithmetic, forward_tables(): return (jnp.cos(phase), jnp.sin(phase))  34.1 us
    dot_general x1, matrix products, spectral_conv(): jnp.dot(cos_inv, prod_cos, precision=exact, preferred_element_type=jnp.fl...  26 us
    dot_general x1, matrix products, spectral_conv(): jnp.dot(sin_inv, prod_sin, precision=exact, preferred_element_type=jnp.fl...  23.7 us
  transfers between devices with their start and end apart: 3, of which 1 were waited for; matrix products, arithmetic and copies ran while one was open for 47% of the time, Pallas kernels for 0%

commit v1 on v0

v1 whole, which is shorter than its diff:
```python
import functools
import math

import jax
import jax.numpy as jnp
import numpy as np
from jax import lax
from jax.experimental import pallas as pl
from jax.experimental.pallas import tpu as pltpu
from jax.sharding import PartitionSpec as P

MESH = pl.DeviceIdType.MESH
WIRE = jnp.bfloat16
GRID = (2, 8, 4, 2)
BLOCKS = 8
CHUNKS = 4


def split_bf16(table):
    high = table.astype(np.float32).astype(jnp.bfloat16)
    low = (table - high.astype(np.float64)).astype(np.float32).astype(jnp.bfloat16)
    return np.stack([high, low])


def tables(block, seqs):
    period = 2 * block
    freq = np.arange(block)[:, None] + 0.5
    place = np.arange(period)[None, :]
    phase = 2.0 * math.pi * freq * place / period
    forward = np.concatenate([np.cos(phase), np.sin(phase)], 0)
    inverse = forward.T[block:] * (2.0 / period)
    taps = np.zeros((2, period, seqs, 2, 8))
    for half in range(2):
        taps[half, :, :, half, :] = forward[:, :block].reshape(period, seqs, 8)
    return (
        split_bf16(forward),
        split_bf16(taps.reshape(2 * period, seqs * 16)),
        split_bf16(inverse),
    )


def layer(
    grid,
    blocks,
    chunks,
    feat_hbm,
    vw_hbm,
    gw_hbm,
    ker_hbm,
    skip_hbm,
    fwd_hbm,
    fker_hbm,
    inv_hbm,
    out_hbm,
    feat,
    wgt,
    ktmp,
    skip,
    fwd,
    fker,
    inv,
    kg,
    vsend,
    vrecv,
    gsend,
    grecv,
    vown,
    gown,
    xs,
    es,
    kh,
    ys,
    conv,
    obuf,
    in_sem,
    feat_sem,
    out_sem,
    v_ssem,
    v_rsem,
    g_ssem,
    g_rsem,
    h_ssem,
    h_rsem,
    a_sem,
    z_ssem,
    z_rsem,
    x_ssem,
    x_rsem,
    c_sem,
):
    n_yh, n_z, n_x, n_core = grid
    n_seq = n_yh * n_z * n_x * n_core
    rows = feat.shape[0]
    size = rows // chunks
    block = rows // blocks
    channels = vown.shape[1]
    seqs = n_seq // blocks

    me = lax.axis_index("seq")
    side = lax.axis_index("ch")
    core = me % n_core
    x = me // n_core % n_x
    z = me // (n_core * n_x) % n_z
    yh = me // (n_core * n_x * n_z)

    def seq_of(yh, z, x, core):
        return ((yh * n_z + z) * n_x + x) * n_core + core

    other = pl.ds(pl.multiple_of((1 - side) * channels, 128), channels)
    own = pl.ds(pl.multiple_of(side * channels, 128), channels)

    def feat_copy(i):
        part = pl.ds(pl.multiple_of(i * size, size), size)
        return pltpu.make_async_copy(feat_hbm.at[part], feat.at[part], feat_sem.at[i])

    weight_copies = [
        pltpu.make_async_copy(hbm.at[:, cols], wgt.at[j], in_sem.at[j])
        for j, (hbm, cols) in enumerate(
            ((vw_hbm, other), (vw_hbm, own), (gw_hbm, other), (gw_hbm, own))
        )
    ]
    small_copies = [
        pltpu.make_async_copy(hbm, ref, in_sem.at[4 + j])
        for j, (hbm, ref) in enumerate(
            (
                (ker_hbm, ktmp),
                (fker_hbm, fker),
                (fwd_hbm, fwd),
                (inv_hbm, inv),
                (skip_hbm, skip),
            )
        )
    ]
    small_copies[0].start()
    feat_copy(0).start()
    weight_copies[0].start()
    for i in range(1, chunks):
        feat_copy(i).start()
    for copy in weight_copies[1:]:
        copy.start()
    for copy in small_copies[1:]:
        copy.start()

    partner = {"ch": 1 - side}
    following = {"seq": (me + 1) % n_seq}
    preceding = {"seq": (me + n_seq - 1) % n_seq}
    yh_partner = {"seq": seq_of(1 - yh, z, x, core)}
    core_partner = {"seq": seq_of(yh, z, x, 1 - core)}
    z_to = {d: {"seq": seq_of(yh, (z + d) % n_z, x, core)} for d in range(1, n_z)}
    x_to = {d: {"seq": seq_of(yh, z, (x + d) % n_x, core)} for d in range(1, n_x)}
    everyone = [partner, following, preceding, yh_partner, core_partner]
    everyone += list(z_to.values()) + list(x_to.values())
    barrier = pltpu.get_barrier_semaphore()
    for device in everyone:
        pl.semaphore_signal(barrier, inc=1, device_id=device, device_id_type=MESH)

    def remote(src, dst, ssem, rsem, device):
        return pltpu.make_async_remote_copy(
            src_ref=src,
            dst_ref=dst,
            send_sem=ssem,
            recv_sem=rsem,
            device_id=device,
            device_id_type=MESH,
        )

    def part(i):
        return pl.ds(pl.multiple_of(i * size, size), size)

    def v_copy(i):
        return remote(vsend.at[part(i)], vrecv.at[part(i)], v_ssem.at[i], v_rsem.at[i], partner)

    def g_copy(i):
        return remote(gsend.at[part(i)], grecv.at[part(i)], g_ssem.at[i], g_rsem.at[i], partner)

    def current(i):
        return pl.ds(pl.multiple_of(rows + i * size, size), size)

    def h_copy(i):
        return remote(xs.at[current(i)], xs.at[part(i)], h_ssem.at[i], h_rsem.at[i], following)

    def a_copy(sender):
        slot = kg.at[core, x, z, sender]
        return remote(slot, slot, a_sem.at[0], a_sem.at[1], yh_partner)

    def z_copy(d, sender):
        slot = kg.at[core, x, sender]
        return remote(slot, slot, z_ssem.at[d], z_rsem.at[d], z_to[d])

    def x_copy(d, sender):
        slot = kg.at[core, sender]
        return remote(slot, slot, x_ssem.at[d], x_rsem.at[d], x_to[d])

    def c_copy(sender):
        slot = kg.at[sender]
        return remote(slot, slot, c_sem.at[0], c_sem.at[1], core_partner)

    small_copies[0].wait()
    taps = ktmp[...].astype(jnp.float32)
    half = channels // 2
    kg[core, x, z, yh] = jnp.concatenate([taps[:, :half], taps[:, half:]], 0).astype(kg.dtype)

    weight_copies[0].wait()

    @pl.loop(0, chunks)
    def _(i):
        feat_copy(i).wait()
        total = jnp.dot(feat[part(i)], wgt[0], preferred_element_type=jnp.float32)
        vsend[part(i)] = total.astype(vsend.dtype)

        @pl.when(i == 0)
        def _():
            pl.semaphore_wait(barrier, len(everyone))
            a_copy(yh).start()

        v_copy(i).start()

    a_copy(1 - yh).wait_recv()
    for d in range(1, n_z):
        z_copy(d, z).start()

    weight_copies[1].wait()

    @pl.loop(0, chunks)
    def _(i):
        vown[part(i)] = jnp.dot(feat[part(i)], wgt[1], preferred_element_type=jnp.float32)

    for d in range(1, n_z):
        z_copy(d, (z + n_z - d) % n_z).wait_recv()
    for d in range(1, n_x):
        x_copy(d, x).start()

    weight_copies[2].wait()

    @pl.loop(0, chunks)
    def _(i):
        total = jnp.dot(feat[part(i)], wgt[2], preferred_element_type=jnp.float32)
        gsend[part(i)] = total.astype(gsend.dtype)

    weight_copies[3].wait()

    @pl.loop(0, chunks)
    def _(i):
        gown[part(i)] = jnp.dot(feat[part(i)], wgt[3], preferred_element_type=jnp.float32)

    for d in range(1, n_x):
        x_copy(d, (x + n_x - d) % n_x).wait_recv()
    c_copy(core).start()

    @pl.loop(0, chunks)
    def _(i):
        v_copy(i).wait_recv()
        total = vown[part(i)] + vrecv[part(i)].astype(jnp.float32)
        xs[current(i)] = total.astype(xs.dtype)

        @pl.when(me < n_seq - 1)
        def _():
            h_copy(i).start()

        @pl.when(i == chunks - 2)
        def _():
            g_copy(0).start()

    for i in range(1, chunks):
        g_copy(i).start()

    c_copy(1 - core).wait_recv()
    for copy in small_copies[1:]:
        copy.wait()
    for p in range(blocks):
        pieces = []
        for seq in range(p * seqs, (p + 1) * seqs):
            at_core, at_x = seq % n_core, seq // n_core % n_x
            at_z, at_yh = seq // (n_core * n_x) % n_z, seq // (n_core * n_x * n_z)
            pieces.append(kg[at_core, at_x, at_z, at_yh])
        taps = jnp.concatenate(pieces, 0)
        kh[p] = jnp.dot(fker[0], taps, preferred_element_type=jnp.float32) + jnp.dot(
            fker[1], taps, preferred_element_type=jnp.float32
        )

    def forward(m):
        pair = xs[pl.ds(pl.multiple_of(m * block, block), 2 * block)]
        es[m] = jnp.dot(fwd[0], pair, preferred_element_type=jnp.float32) + jnp.dot(
            fwd[1], pair, preferred_element_type=jnp.float32
        )

    pl.loop(blocks, 2 * blocks - 1)(forward)

    @pl.when(me == 0)
    def _():
        xs[pl.ds(0, rows)] = jnp.zeros((rows, channels), xs.dtype)

    @pl.when(me > 0)
    def _():
        for i in range(chunks):
            h_copy(i).wait_recv()

    pl.loop(0, blocks)(forward)

    @pl.loop(0, block // 8)
    def _(r):
        real = pl.ds(pl.multiple_of(r * 8, 8), 8)
        imag = pl.ds(pl.multiple_of(block + r * 8, 8), 8)
        for part_of in range(2):
            lanes = pl.ds(part_of * half, half)
            at = part_of * 2 * block
            k_real = [kh[p, pl.ds(pl.multiple_of(at + r * 8, 8), 8)] for p in range(blocks)]
            k_imag = [kh[p, pl.ds(pl.multiple_of(at + block + r * 8, 8), 8)] for p in range(blocks)]
            sum_real = [None] * blocks
            sum_imag = [None] * blocks
            for m in range(2 * blocks - 1):
                e_real, e_imag = es[m, real, lanes], es[m, imag, lanes]
                for a in range(blocks):
                    p = blocks - 1 + a - m
                    if not 0 <= p < blocks:
                        continue
                    new_real = e_real * k_real[p] - e_imag * k_imag[p]
                    new_imag = e_imag * k_real[p] + e_real * k_imag[p]
                    if sum_real[a] is None:
                        sum_real[a], sum_imag[a] = new_real, new_imag
                    else:
                        sum_real[a], sum_imag[a] = sum_real[a] + new_real, sum_imag[a] + new_imag
            for a in range(blocks):
                ys[a, real, lanes] = sum_real[a]
                ys[a, imag, lanes] = sum_imag[a]

    gain = skip[...]

    @pl.loop(0, blocks)
    def _(a):
        spectrum = ys[a]
        high = spectrum.astype(jnp.bfloat16)
        low = (spectrum - high.astype(jnp.float32)).astype(jnp.bfloat16)
        back = (
            jnp.dot(inv[0], high, preferred_element_type=jnp.float32)
            + jnp.dot(inv[1], high, preferred_element_type=jnp.float32)
            + jnp.dot(inv[0], low, preferred_element_type=jnp.float32)
        )
        direct = xs[pl.ds(pl.multiple_of(rows + a * block, block), block)].astype(jnp.float32)
        conv[pl.ds(pl.multiple_of(a * block, block), block)] = back + gain * direct

    def out_copy(i):
        return pltpu.make_async_copy(obuf.at[part(i)], out_hbm.at[part(i)], out_sem.at[i])

    @pl.loop(0, chunks)
    def _(i):
        g_copy(i).wait_recv()
        gate = gown[part(i)] + grecv[part(i)].astype(jnp.float32)
        obuf[part(i)] = (conv[part(i)] * (gate / (1.0 + jnp.exp(-gate)))).astype(obuf.dtype)
        out_copy(i).start()

    for i in range(chunks):
        v_copy(i).wait_send()
        g_copy(i).wait_send()

    @pl.when(me < n_seq - 1)
    def _():
        for i in range(chunks):
            h_copy(i).wait_send()

    a_copy(yh).wait_send()
    for d in range(1, n_z):
        z_copy(d, z).wait_send()
    for d in range(1, n_x):
        x_copy(d, x).wait_send()
    c_copy(core).wait_send()
    for i in range(chunks):
        out_copy(i).wait()


def solution(mesh, grid=GRID, blocks=BLOCKS, chunks=CHUNKS):
    def on_device(features, value_weight, gate_weight, kernel, skip_gain):
        rows, depth = features.shape
        tap_rows, channels = kernel.shape
        n_seq = math.prod(grid)
        block = rows // blocks
        seqs = n_seq // blocks
        fwd, fker, inv = tables(block, seqs)
        f32, bf16 = jnp.float32, jnp.bfloat16
        dma = pltpu.SemaphoreType.DMA
        n_yh, n_z, n_x, n_core = grid
        return pl.pallas_call(
            functools.partial(layer, grid, blocks, chunks),
            out_shape=jax.ShapeDtypeStruct((rows, channels), bf16),
            in_specs=[pl.BlockSpec(memory_space=pl.ANY)] * 8,
            out_specs=pl.BlockSpec(memory_space=pl.ANY),
            scratch_shapes=[
                pltpu.VMEM((rows, depth), bf16),
                pltpu.VMEM((4, depth, channels), bf16),
                pltpu.VMEM((tap_rows, channels), bf16),
                pltpu.VMEM((1, channels), f32),
                pltpu.VMEM(fwd.shape, bf16),
                pltpu.VMEM(fker.shape, bf16),
                pltpu.VMEM(inv.shape, bf16),
                pltpu.VMEM((n_core, n_x, n_z, n_yh, 2 * tap_rows, channels // 2), bf16),
                pltpu.VMEM((rows, channels), WIRE),
                pltpu.VMEM((rows, channels), WIRE),
                pltpu.VMEM((rows, channels), WIRE),
                pltpu.VMEM((rows, channels), WIRE),
                pltpu.VMEM((rows, channels), f32),
                pltpu.VMEM((rows, channels), f32),
                pltpu.VMEM((2 * rows, channels), bf16),
                pltpu.VMEM((2 * blocks - 1, 2 * block, channels), f32),
                pltpu.VMEM((blocks, 4 * block, channels // 2), f32),
                pltpu.VMEM((blocks, 2 * block, channels), f32),
                pltpu.VMEM((rows, channels), f32),
                pltpu.VMEM((rows, channels), bf16),
                dma((9,)),
                dma((chunks,)),
                dma((chunks,)),
                dma((chunks,)),
                dma((chunks,)),
                dma((chunks,)),
                dma((chunks,)),
                dma((chunks,)),
                dma((chunks,)),
                dma((2,)),
                dma((n_z,)),
                dma((n_z,)),
                dma((n_x,)),
                dma((n_x,)),
                dma((2,)),
            ],
            compiler_params=pltpu.CompilerParams(
                collective_id=0, has_side_effects=True, vmem_limit_bytes=56 * 2**20
            ),
            cost_estimate=pl.CostEstimate(
                flops=8 * rows * depth * channels,
                bytes_accessed=2 * (rows * depth + 4 * depth * channels + rows * channels),
                transcendentals=rows * channels,
            ),
        )(
            features,
            value_weight,
            gate_weight,
            kernel,
            skip_gain.reshape(1, channels),
            jnp.asarray(fwd),
            jnp.asarray(fker),
            jnp.asarray(inv),
        )

    return jax.shard_map(
        on_device,
        mesh=mesh,
        in_specs=(P("seq", "ch"), P("ch", None), P("ch", None), P("seq", "ch"), P("ch")),
        out_specs=P("seq", "ch"),
        check_vma=False,
    )
```

time: 469 us -> 41.6 us (0.09)
  the two profiles are of different devices: /device:TPU:24 before, /device:TPU:8 now
where the time goes in v1:
time: 41.6 us; the launch traced here: 41.5 us
  Pallas kernels  39.6 us (95%)
  local copies, waits for them, and re-layouts  1.87 us (4%)
    pallas_call x1, Pallas kernels, on_device(): pl.pallas_call(functools.partial(layer, grid, blocks, chunks), out_shape=...  39.6 us
    unnamed x1, local copies, waits for them, and re-layouts  1.87 us

profile of v1, /device:TPU:8, one launch (start us, length us, event | category | flops | bytes accessed | tf_op | source)
XLA Modules:
  0.0 41.5 jit_solution(16674329471944942046)
XLA Ops:
  0.0 39.6 %shard_map.82 = bf16[1024,256]{1,0:T(8,128)(2,1)} custom-call(bf16[1024,2048]{1,0:T(8,128)(2,1)} %feat_hbm.1, bf16[2048,512]{1,0:T(8,128)(2,1)} %vw_hbm.1, bf16[2048,512]{1,0:T(8,128)(2,1)} %gw_hbm.1, bf16[8,256]{1,0:T(8,128)(2,1)} %ker_hbm.1, f32[1,256]{1,0:T(1,128)} %bitcast.1, bf16[2,256,256]{2,1,0:T(8,128)(2,1)} %constant.6.clone.fwd_hbm, ...), custom_call_target="tpu_custom_call" | custom-call | flops 4294967296 | bytes 8912896 | tf_op jit(solution)/shard_map/pallas_call | solution.py:382
  39.6 1.9 %copy.10 = bf16[1024,256]{1,0:T(8,128)(2,1)} copy(bf16[1024,256]{1,0:T(8,128)(2,1)} %shard_map.82) | data formatting | bytes 1048576

commit v2 on v1

v2 whole, which is shorter than its diff:
```python
import functools
import math

import jax
import jax.numpy as jnp
import numpy as np
from jax import lax
from jax.experimental import pallas as pl
from jax.experimental.pallas import tpu as pltpu
from jax.sharding import PartitionSpec as P

MESH = pl.DeviceIdType.MESH
WIRE = jnp.bfloat16
GRID = (2, 8, 4, 2)
BLOCKS = 8
CHUNKS = 4


def tables(block):
    period = 2 * block
    freq = np.arange(block)[:, None] + 0.5
    place = np.arange(period)[None, :]
    phase = 2.0 * math.pi * freq * place / period
    forward = np.concatenate([np.cos(phase), np.sin(phase)], 0)
    inverse = forward.T[block:] * (2.0 / period)
    return forward.astype(jnp.bfloat16), inverse.astype(jnp.bfloat16)


def layer(
    grid,
    blocks,
    chunks,
    feat_hbm,
    vw_hbm,
    gw_hbm,
    ker_hbm,
    skip_hbm,
    fwd_hbm,
    inv_hbm,
    out,
    feat,
    wgt,
    ktmp,
    skip,
    fwd,
    inv,
    kg,
    vsend,
    vrecv,
    gsend,
    grecv,
    vown,
    gown,
    xs,
    es,
    kh,
    ys,
    conv,
    relay,
    in_sem,
    feat_sem,
    v_ssem,
    v_rsem,
    g_ssem,
    g_rsem,
    h_ssem,
    h_rsem,
    a_sem,
    z_ssem,
    z_rsem,
    x_ssem,
    x_rsem,
    c_sem,
    s_sem,
    r_sem,
    q_sem,
    d_sem,
):
    n_yh, n_z, n_x, n_core = grid
    n_seq = n_yh * n_z * n_x * n_core
    rows = feat.shape[0]
    size = rows // chunks
    block = rows // blocks
    channels = vown.shape[1]
    seqs = n_seq // blocks

    me = lax.axis_index("seq")
    side = lax.axis_index("ch")
    core = me % n_core
    x = me // n_core % n_x
    z = me // (n_core * n_x) % n_z
    yh = me // (n_core * n_x * n_z)

    def seq_of(yh, z, x, core):
        return ((yh * n_z + z) * n_x + x) * n_core + core

    other = pl.ds(pl.multiple_of((1 - side) * channels, 128), channels)
    own = pl.ds(pl.multiple_of(side * channels, 128), channels)

    def feat_copy(i):
        part = pl.ds(pl.multiple_of(i * size, size), size)
        return pltpu.make_async_copy(feat_hbm.at[part], feat.at[part], feat_sem.at[i])

    weight_copies = [
        pltpu.make_async_copy(hbm.at[:, cols], wgt.at[j], in_sem.at[j])
        for j, (hbm, cols) in enumerate(
            ((vw_hbm, other), (vw_hbm, own), (gw_hbm, other), (gw_hbm, own))
        )
    ]
    small_copies = [
        pltpu.make_async_copy(hbm, ref, in_sem.at[4 + j])
        for j, (hbm, ref) in enumerate(
            (
                (ker_hbm, ktmp),
                (fwd_hbm, fwd),
                (inv_hbm, inv),
                (skip_hbm, skip),
            )
        )
    ]
    small_copies[0].start()
    feat_copy(0).start()
    weight_copies[0].start()
    for i in range(1, chunks):
        feat_copy(i).start()
    for copy in weight_copies[1:]:
        copy.start()
    for copy in small_copies[1:]:
        copy.start()

    partner = {"ch": 1 - side}
    following = {"seq": (me + 1) % n_seq}
    preceding = {"seq": (me + n_seq - 1) % n_seq}
    yh_partner = {"seq": seq_of(1 - yh, z, x, core)}
    core_partner = {"seq": seq_of(yh, z, x, 1 - core)}
    z_to = {d: {"seq": seq_of(yh, (z + d) % n_z, x, core)} for d in range(1, n_z)}
    x_to = {d: {"seq": seq_of(yh, z, (x + d) % n_x, core)} for d in range(1, n_x)}
    source, target = n_seq // 2 - 1, n_seq // 2
    at_end = (x == n_x - 1) & (core == n_core - 1)
    is_source = me == source
    is_first = at_end & (yh == 0) & (z < n_z - 1)
    at_seam = at_end & (yh == 0)
    is_second = at_end & (yh == 1)
    piece_rows = rows // n_z
    sends_halo = (me < n_seq - 1) & (me != source)
    gets_halo = (me > 0) & (me != target)

    late = n_z // 2
    others = [(z + d) % n_z for d in range(1, n_z)]
    z_devices = [{"seq": seq_of(yh, other, x, core)} for other in others]
    is_later = [(z < late) & (other > z) for other in others]
    is_earlier = [(other < late) & (other < z) for other in others]
    is_level = [(z >= late) & (other >= late) for other in others]
    leads = (core == n_core - 1) & sends_halo
    led = (core == 0) & gets_halo
    barrier = pltpu.get_barrier_semaphore()

    def signal(device):
        pl.semaphore_signal(barrier, inc=1, device_id=device, device_id_type=MESH)

    def signal_if(condition, device):
        @pl.when(condition)
        def _():
            signal(device)

    level = [partner, core_partner, yh_partner] + list(x_to.values())
    level_count = len(level)
    for device in level:
        signal(device)
    for device, condition in zip(z_devices, is_level):
        signal_if(condition, device)
    signal_if(led, preceding)

    @pl.when(me == target)
    def _():
        for j in range(n_z):
            signal({"seq": seq_of(1, j, n_x - 1, n_core - 1)})

    def count(*conditions):
        return sum(condition.astype(jnp.int32) for condition in conditions)

    def enter():
        pl.semaphore_wait(
            barrier,
            level_count
            + jnp.where(z < late, z, n_z - 1)
            + count(leads, is_second),
        )
        for device, later, earlier in zip(z_devices, is_later, is_earlier):
            signal_if(later | earlier, device)

    def hear_answers():
        pl.semaphore_wait(barrier, n_z - 1 - z)

    def remote(src, dst, ssem, rsem, device):
        return pltpu.make_async_remote_copy(
            src_ref=src,
            dst_ref=dst,
            send_sem=ssem,
            recv_sem=rsem,
            device_id=device,
            device_id_type=MESH,
        )

    def part(i):
        return pl.ds(pl.multiple_of(i * size, size), size)

    def v_copy(i):
        return remote(vsend.at[part(i)], vrecv.at[part(i)], v_ssem.at[i], v_rsem.at[i], partner)

    def g_copy(i):
        return remote(gsend.at[part(i)], grecv.at[part(i)], g_ssem.at[i], g_rsem.at[i], partner)

    def current(i):
        return pl.ds(pl.multiple_of(rows + i * size, size), size)

    def h_copy(i):
        return remote(xs.at[current(i)], xs.at[part(i)], h_ssem.at[i], h_rsem.at[i], following)

    def piece(j, start):
        return pl.ds(pl.multiple_of(start + j * piece_rows, piece_rows), piece_rows)

    def seam_first(j):
        device = {"seq": seq_of(0, j, n_x - 1, n_core - 1)}
        return remote(xs.at[piece(j, rows)], relay, s_sem.at[j], r_sem.at[0], device)

    def seam_last():
        return remote(xs.at[piece(n_z - 1, rows)], relay, r_sem.at[1], q_sem.at[0], yh_partner)

    def seam_second():
        return remote(relay, relay, r_sem.at[1], q_sem.at[0], yh_partner)

    def seam_third(j):
        return remote(relay, xs.at[piece(j, 0)], q_sem.at[1], d_sem.at[j], {"seq": target})

    def a_copy(sender):
        slot = kg.at[core, x, z, sender]
        return remote(slot, slot, a_sem.at[0], a_sem.at[1], yh_partner)

    def z_copy(d, sender):
        slot = kg.at[core, x, sender]
        return remote(slot, slot, z_ssem.at[d], z_rsem.at[d], z_to[d])

    def x_copy(d, sender):
        slot = kg.at[core, sender]
        return remote(slot, slot, x_ssem.at[d], x_rsem.at[d], x_to[d])

    def c_copy(sender):
        slot = kg.at[sender]
        return remote(slot, slot, c_sem.at[0], c_sem.at[1], core_partner)

    small_copies[0].wait()
    taps = ktmp[...].astype(jnp.float32)
    half = channels // 2
    kg[core, x, z, yh] = jnp.concatenate([taps[:, :half], taps[:, half:]], 0).astype(kg.dtype)

    weight_copies[0].wait()

    @pl.loop(0, chunks)
    def _(i):
        feat_copy(i).wait()
        total = jnp.dot(feat[part(i)], wgt[0], preferred_element_type=jnp.float32)
        vsend[part(i)] = total.astype(vsend.dtype)

        @pl.when(i == 0)
        def _():
            enter()
            a_copy(yh).start()

        v_copy(i).start()

    a_copy(1 - yh).wait_recv()

    @pl.when(z >= late)
    def _():
        for d in range(1, n_z):
            z_copy(d, z).start()

    weight_copies[1].wait()

    @pl.loop(0, chunks)
    def _(i):
        vown[part(i)] = jnp.dot(feat[part(i)], wgt[1], preferred_element_type=jnp.float32)

    weight_copies[2].wait()

    @pl.loop(0, chunks)
    def _(i):
        total = jnp.dot(feat[part(i)], wgt[2], preferred_element_type=jnp.float32)
        gsend[part(i)] = total.astype(gsend.dtype)

    @pl.when(z < late)
    def _():
        hear_answers()
        for d in range(1, n_z):
            z_copy(d, z).start()

    weight_copies[3].wait()

    @pl.loop(0, chunks)
    def _(i):
        gown[part(i)] = jnp.dot(feat[part(i)], wgt[3], preferred_element_type=jnp.float32)

    for d in range(1, n_z):
        z_copy(d, (z + n_z - d) % n_z).wait_recv()
    for d in range(1, n_x):
        x_copy(d, x).start()

    def arrived(i):
        v_copy(i).wait_recv()
        total = vown[part(i)] + vrecv[part(i)].astype(jnp.float32)
        xs[current(i)] = total.astype(xs.dtype)

        @pl.when(sends_halo)
        def _():
            h_copy(i).start()

        @pl.when(is_source)
        def _():
            for j in range(i * n_z // chunks, (i + 1) * n_z // chunks):
                if j < n_z - 1:
                    seam_first(j).start()
                else:
                    seam_last().start()

    for i in range(chunks):
        arrived(i)
        if i == chunks - 2:

            @pl.when(jnp.logical_not(at_seam))
            def _():
                g_copy(0).start()

    @pl.when(is_first)
    def _():
        seam_first(z).wait_recv()
        seam_second().start()

    @pl.when(at_seam)
    def _():
        g_copy(0).start()

    for i in range(1, chunks):
        g_copy(i).start()

    def forward(m):
        pair = xs[pl.ds(pl.multiple_of(m * block, block), 2 * block)]
        es[m] = jnp.dot(fwd[...], pair, preferred_element_type=jnp.float32)

    def products(first, last):
        more = first == 0

        @pl.loop(0, block // 8)
        def _(r):
            real = pl.ds(pl.multiple_of(r * 8, 8), 8)
            imag = pl.ds(pl.multiple_of(block + r * 8, 8), 8)
            for part_of in range(2):
                lanes = pl.ds(part_of * half, half)
                k_real = [kh[p, real, lanes] for p in range(blocks)]
                k_imag = [kh[p, imag, lanes] for p in range(blocks)]
                sum_real = [ys[a, real, lanes] if more and a else None for a in range(blocks)]
                sum_imag = [ys[a, imag, lanes] if more and a else None for a in range(blocks)]
                for m in range(first, last):
                    e_real, e_imag = es[m, real, lanes], es[m, imag, lanes]
                    for a in range(blocks):
                        p = blocks - 1 + a - m
                        if not 0 <= p < blocks:
                            continue
                        new_real = e_real * k_real[p] - e_imag * k_imag[p]
                        new_imag = e_imag * k_real[p] + e_real * k_imag[p]
                        if sum_real[a] is None:
                            sum_real[a], sum_imag[a] = new_real, new_imag
                        else:
                            sum_real[a] = sum_real[a] + new_real
                            sum_imag[a] = sum_imag[a] + new_imag
                for a in range(blocks):
                    if sum_real[a] is not None:
                        ys[a, real, lanes] = sum_real[a]
                        ys[a, imag, lanes] = sum_imag[a]

    def transform_taps():
        c_copy(1 - core).wait_recv()
        for p in range(blocks):
            pieces = []
            for seq in range(p * seqs, (p + 1) * seqs):
                at_core, at_x = seq % n_core, seq // n_core % n_x
                at_z, at_yh = seq // (n_core * n_x) % n_z, seq // (n_core * n_x * n_z)
                taps = kg[at_core, at_x, at_z, at_yh].astype(jnp.float32)
                pieces.append(jnp.concatenate([taps[:8], taps[8:]], 1))
            taps = jnp.concatenate(pieces, 0).astype(jnp.bfloat16)
            kh[p] = jnp.dot(fwd[:, :block], taps, preferred_element_type=jnp.float32)

    def transform_halo():
        done = 0
        for i in range(chunks):

            @pl.when(gets_halo)
            def _():
                h_copy(i).wait_recv()

            @pl.when(me == target)
            def _():
                for j in range(i * n_z // chunks, (i + 1) * n_z // chunks):
                    seam_third(j).wait_recv()

            ready = blocks if i == chunks - 1 else (i + 1) * blocks // chunks - 1
            pl.loop(done, ready)(forward)
            done = ready

    for copy in small_copies[1:]:
        copy.wait()
    pl.loop(blocks, 2 * blocks - 1)(forward)
    for d in range(1, n_x):
        x_copy(d, (x + n_x - d) % n_x).wait_recv()
    c_copy(core).start()

    @pl.when(me == 0)
    def _():
        xs[pl.ds(0, rows)] = jnp.zeros((rows, channels), xs.dtype)

    @pl.when(is_second)
    def _():
        seam_second().wait_recv()
        seam_third(z).start()

    taps_last = (z < late) & (me != target)

    @pl.when(taps_last)
    def _():
        transform_halo()
        transform_taps()
        products(blocks, 2 * blocks - 1)

    @pl.when(jnp.logical_not(taps_last))
    def _():
        transform_taps()
        products(blocks, 2 * blocks - 1)
        transform_halo()

    products(0, blocks)

    gain = skip[...]

    @pl.loop(0, blocks)
    def _(a):
        spectrum = ys[a].astype(jnp.bfloat16)
        back = jnp.dot(inv[...], spectrum, preferred_element_type=jnp.float32)
        direct = xs[pl.ds(pl.multiple_of(rows + a * block, block), block)].astype(jnp.float32)
        conv[pl.ds(pl.multiple_of(a * block, block), block)] = back + gain * direct

    @pl.loop(0, chunks)
    def _(i):
        g_copy(i).wait_recv()
        gate = gown[part(i)] + grecv[part(i)].astype(jnp.float32)
        out[part(i)] = (conv[part(i)] * (gate / (1.0 + jnp.exp(-gate)))).astype(out.dtype)

    for i in range(chunks):
        v_copy(i).wait_send()
        g_copy(i).wait_send()

    @pl.when(sends_halo)
    def _():
        for i in range(chunks):
            h_copy(i).wait_send()

    a_copy(yh).wait_send()
    for d in range(1, n_z):
        z_copy(d, z).wait_send()
    for d in range(1, n_x):
        x_copy(d, x).wait_send()
    c_copy(core).wait_send()

    @pl.when(is_source)
    def _():
        for j in range(n_z - 1):
            seam_first(j).wait_send()
        seam_last().wait_send()

    @pl.when(is_first)
    def _():
        seam_second().wait_send()

    @pl.when(is_second)
    def _():
        seam_third(z).wait_send()


def solution(mesh, grid=GRID, blocks=BLOCKS, chunks=CHUNKS):
    def on_device(features, value_weight, gate_weight, kernel, skip_gain):
        rows, depth = features.shape
        tap_rows, channels = kernel.shape
        block = rows // blocks
        fwd, inv = tables(block)
        f32, bf16 = jnp.float32, jnp.bfloat16
        dma = pltpu.SemaphoreType.DMA
        n_yh, n_z, n_x, n_core = grid
        return pl.pallas_call(
            functools.partial(layer, grid, blocks, chunks),
            out_shape=pltpu.VMEM((rows, channels), bf16),
            in_specs=[pl.BlockSpec(memory_space=pl.ANY)] * 7,
            out_specs=pl.BlockSpec(memory_space=pltpu.VMEM),
            scratch_shapes=[
                pltpu.VMEM((rows, depth), bf16),
                pltpu.VMEM((4, depth, channels), bf16),
                pltpu.VMEM((tap_rows, channels), bf16),
                pltpu.VMEM((1, channels), f32),
                pltpu.VMEM(fwd.shape, bf16),
                pltpu.VMEM(inv.shape, bf16),
                pltpu.VMEM((n_core, n_x, n_z, n_yh, 2 * tap_rows, channels // 2), bf16),
                pltpu.VMEM((rows, channels), WIRE),
                pltpu.VMEM((rows, channels), WIRE),
                pltpu.VMEM((rows, channels), WIRE),
                pltpu.VMEM((rows, channels), WIRE),
                pltpu.VMEM((rows, channels), f32),
                pltpu.VMEM((rows, channels), f32),
                pltpu.VMEM((2 * rows, channels), bf16),
                pltpu.VMEM((2 * blocks - 1, 2 * block, channels), f32),
                pltpu.VMEM((blocks, 2 * block, channels), f32),
                pltpu.VMEM((blocks, 2 * block, channels), f32),
                pltpu.VMEM((rows, channels), f32),
                pltpu.VMEM((rows // n_z, channels), bf16),
                dma((9,)),
                dma((chunks,)),
                dma((chunks,)),
                dma((chunks,)),
                dma((chunks,)),
                dma((chunks,)),
                dma((chunks,)),
                dma((chunks,)),
                dma((2,)),
                dma((n_z,)),
                dma((n_z,)),
                dma((n_x,)),
                dma((n_x,)),
                dma((2,)),
                dma((n_z,)),
                dma((2,)),
                dma((2,)),
                dma((n_z,)),
            ],
            compiler_params=pltpu.CompilerParams(
                collective_id=0, has_side_effects=True, vmem_limit_bytes=56 * 2**20
            ),
            cost_estimate=pl.CostEstimate(
                flops=8 * rows * depth * channels,
                bytes_accessed=2 * (rows * depth + 4 * depth * channels + rows * channels),
                transcendentals=rows * channels,
            ),
        )(
            features,
            value_weight,
            gate_weight,
            kernel,
            skip_gain.reshape(1, channels),
            jnp.asarray(fwd),
            jnp.asarray(inv),
        )

    return jax.shard_map(
        on_device,
        mesh=mesh,
        in_specs=(P("seq", "ch"), P("ch", None), P("ch", None), P("seq", "ch"), P("ch")),
        out_specs=P("seq", "ch"),
        check_vma=False,
    )
```

time: 41.6 us -> 38.9 us (0.935)
  the two profiles are of different devices: /device:TPU:8 before, /device:TPU:24 now
where the time goes in v2:
time: 38.9 us; the launch traced here: 38.5 us
  Pallas kernels  37.7 us (97%)
  local copies, waits for them, and re-layouts  0.8 us (2%)
    pallas_call x1, Pallas kernels, on_device(): pl.pallas_call(functools.partial(layer, grid, blocks, chunks), out_shape=...  37.7 us
    unnamed x1, local copies, waits for them, and re-layouts  0.8 us

profile of v2, /device:TPU:24, one launch (start us, length us, event | category | flops | bytes accessed | tf_op | source)
XLA Modules:
  0.0 38.5 jit_solution(6897617976863604632)
XLA Ops:
  0.0 37.7 %shard_map.73 = bf16[1024,256]{1,0:T(8,128)(2,1)S(1)} custom-call(bf16[1024,2048]{1,0:T(8,128)(2,1)} %feat_hbm.1, bf16[2048,512]{1,0:T(8,128)(2,1)} %vw_hbm.1, bf16[2048,512]{1,0:T(8,128)(2,1)} %gw_hbm.1, bf16[8,256]{1,0:T(8,128)(2,1)} %ker_hbm.1, f32[1,256]{1,0:T(1,128)} %bitcast.1, bf16[256,256]{1,0:T(8,128)(2,1)} %constant.4.clone.fwd_hbm, ...), custom_call_target="tpu_custom_call" | custom-call | flops 4294967296 | bytes 8912896 | tf_op jit(solution)/shard_map/pallas_call | solution.py:497
  37.7 0.8 %copy.9 = bf16[1024,256]{1,0:T(8,128)(2,1)} copy(bf16[1024,256]{1,0:T(8,128)(2,1)S(1)} %shard_map.73) | data formatting | bytes 1048576

commit v3 on v2

--- a/solution.py
+++ b/solution.py
@@ -73,7 +73,6 @@
     c_sem,
     s_sem,
     r_sem,
-    q_sem,
     d_sem,
 ):
     n_yh, n_z, n_x, n_core = grid
@@ -138,9 +137,7 @@
     source, target = n_seq // 2 - 1, n_seq // 2
     at_end = (x == n_x - 1) & (core == n_core - 1)
     is_source = me == source
-    is_first = at_end & (yh == 0) & (z < n_z - 1)
-    at_seam = at_end & (yh == 0)
-    is_second = at_end & (yh == 1)
+    relays = at_end & (yh == 1)
     piece_rows = rows // n_z
     sends_halo = (me < n_seq - 1) & (me != source)
     gets_halo = (me > 0) & (me != target)
@@ -176,6 +173,8 @@
         for j in range(n_z):
             signal({"seq": seq_of(1, j, n_x - 1, n_core - 1)})
 
+    signal_if(relays, {"seq": source})
+
     def count(*conditions):
         return sum(condition.astype(jnp.int32) for condition in conditions)
 
@@ -184,7 +183,8 @@
             barrier,
             level_count
             + jnp.where(z < late, z, n_z - 1)
-            + count(leads, is_second),
+            + count(leads, relays)
+            + jnp.where(is_source, n_z, 0),
         )
         for device, later, earlier in zip(z_devices, is_later, is_earlier):
             signal_if(later | earlier, device)
@@ -221,17 +221,11 @@
         return pl.ds(pl.multiple_of(start + j * piece_rows, piece_rows), piece_rows)
 
     def seam_first(j):
-        device = {"seq": seq_of(0, j, n_x - 1, n_core - 1)}
+        device = {"seq": seq_of(1, j, n_x - 1, n_core - 1)}
         return remote(xs.at[piece(j, rows)], relay, s_sem.at[j], r_sem.at[0], device)
 
-    def seam_last():
-        return remote(xs.at[piece(n_z - 1, rows)], relay, r_sem.at[1], q_sem.at[0], yh_partner)
-
-    def seam_second():
-        return remote(relay, relay, r_sem.at[1], q_sem.at[0], yh_partner)
-
-    def seam_third(j):
-        return remote(relay, xs.at[piece(j, 0)], q_sem.at[1], d_sem.at[j], {"seq": target})
+    def seam_second(j):
+        return remote(relay, xs.at[piece(j, 0)], r_sem.at[1], d_sem.at[j], {"seq": target})
 
     def a_copy(sender):
         slot = kg.at[core, x, z, sender]
@@ -269,6 +263,20 @@
 
         v_copy(i).start()
 
+    def arrived(i):
+        v_copy(i).wait_recv()
+        total = vown[part(i)] + vrecv[part(i)].astype(jnp.float32)
+        xs[current(i)] = total.astype(xs.dtype)
+
+        @pl.when(sends_halo)
+        def _():
+            h_copy(i).start()
+
+        @pl.when(is_source)
+        def _():
+            for j in range(i * n_z // chunks, (i + 1) * n_z // chunks):
+                seam_first(j).start()
+
     a_copy(1 - yh).wait_recv()
 
     @pl.when(z >= late)
@@ -281,6 +289,10 @@
     @pl.loop(0, chunks)
     def _(i):
         vown[part(i)] = jnp.dot(feat[part(i)], wgt[1], preferred_element_type=jnp.float32)
+
+    early = chunks - 2
+    for i in range(early // 2):
+        arrived(i)
 
     weight_copies[2].wait()
 
@@ -289,6 +301,9 @@
         total = jnp.dot(feat[part(i)], wgt[2], preferred_element_type=jnp.float32)
         gsend[part(i)] = total.astype(gsend.dtype)
 
+    for i in range(early // 2, early):
+        arrived(i)
+
     @pl.when(z < late)
     def _():
         hear_answers()
@@ -300,48 +315,24 @@
     @pl.loop(0, chunks)
     def _(i):
         gown[part(i)] = jnp.dot(feat[part(i)], wgt[3], preferred_element_type=jnp.float32)
+
+    arrived(chunks - 2)
+    g_copy(0).start()
 
     for d in range(1, n_z):
         z_copy(d, (z + n_z - d) % n_z).wait_recv()
     for d in range(1, n_x):
         x_copy(d, x).start()
 
-    def arrived(i):
-        v_copy(i).wait_recv()
-        total = vown[part(i)] + vrecv[part(i)].astype(jnp.float32)
-        xs[current(i)] = total.astype(xs.dtype)
-
-        @pl.when(sends_halo)
-        def _():
-            h_copy(i).start()
-
-        @pl.when(is_source)
-        def _():
-            for j in range(i * n_z // chunks, (i + 1) * n_z // chunks):
-                if j < n_z - 1:
-                    seam_first(j).start()
-                else:
-                    seam_last().start()
-
-    for i in range(chunks):
-        arrived(i)
-        if i == chunks - 2:
-
-            @pl.when(jnp.logical_not(at_seam))
-            def _():
-                g_copy(0).start()
-
-    @pl.when(is_first)
-    def _():
-        seam_first(z).wait_recv()
-        seam_second().start()
-
-    @pl.when(at_seam)
-    def _():
-        g_copy(0).start()
+    arrived(chunks - 1)
 
     for i in range(1, chunks):
         g_copy(i).start()
+
+    @pl.when(relays)
+    def _():
+        seam_first(z).wait_recv()
+        seam_second(z).start()
 
     def forward(m):
         pair = xs[pl.ds(pl.multiple_of(m * block, block), 2 * block)]
@@ -401,7 +392,7 @@
             @pl.when(me == target)
             def _():
                 for j in range(i * n_z // chunks, (i + 1) * n_z // chunks):
-                    seam_third(j).wait_recv()
+                    seam_second(j).wait_recv()
 
             ready = blocks if i == chunks - 1 else (i + 1) * blocks // chunks - 1
             pl.loop(done, ready)(forward)
@@ -410,6 +401,7 @@
     for copy in small_copies[1:]:
         copy.wait()
     pl.loop(blocks, 2 * blocks - 1)(forward)
+
     for d in range(1, n_x):
         x_copy(d, (x + n_x - d) % n_x).wait_recv()
     c_copy(core).start()
@@ -417,11 +409,6 @@
     @pl.when(me == 0)
     def _():
         xs[pl.ds(0, rows)] = jnp.zeros((rows, channels), xs.dtype)
-
-    @pl.when(is_second)
-    def _():
-        seam_second().wait_recv()
-        seam_third(z).start()
 
     taps_last = (z < late) & (me != target)
 
@@ -472,17 +459,12 @@
 
     @pl.when(is_source)
     def _():
-        for j in range(n_z - 1):
+        for j in range(n_z):
             seam_first(j).wait_send()
-        seam_last().wait_send()
-
-    @pl.when(is_first)
-    def _():
-        seam_second().wait_send()
-
-    @pl.when(is_second)
-    def _():
-        seam_third(z).wait_send()
+
+    @pl.when(relays)
+    def _():
+        seam_second(z).wait_send()
 
 
 def solution(mesh, grid=GRID, blocks=BLOCKS, chunks=CHUNKS):
@@ -535,7 +517,6 @@
                 dma((2,)),
                 dma((n_z,)),
                 dma((2,)),
-                dma((2,)),
                 dma((n_z,)),
             ],
             compiler_params=pltpu.CompilerParams(

time: 38.9 us -> 35.9 us (0.923)
  Pallas kernels: 37.7 us -> 35 us
    pallas_call x1, Pallas kernels: 37.7 us -> 35 us  [on_device(): pl.pallas_call(functools.partial(layer, grid, blocks, chunks), out_shape=...]
where the time goes in v3:
time: 35.9 us; the launch traced here: 35.8 us
  Pallas kernels  35 us (97%)
  local copies, waits for them, and re-layouts  0.8 us (2%)
    pallas_call x1, Pallas kernels, on_device(): pl.pallas_call(functools.partial(layer, grid, blocks, chunks), out_shape=...  35 us
    unnamed x1, local copies, waits for them, and re-layouts  0.8 us

profile of v3, /device:TPU:24, one launch (start us, length us, event | category | flops | bytes accessed | tf_op | source)
XLA Modules:
  0.0 35.8 jit_solution(84227376810378717)
XLA Ops:
  0.0 35.0 %shard_map.73 = bf16[1024,256]{1,0:T(8,128)(2,1)S(1)} custom-call(bf16[1024,2048]{1,0:T(8,128)(2,1)} %feat_hbm.1, bf16[2048,512]{1,0:T(8,128)(2,1)} %vw_hbm.1, bf16[2048,512]{1,0:T(8,128)(2,1)} %gw_hbm.1, bf16[8,256]{1,0:T(8,128)(2,1)} %ker_hbm.1, f32[1,256]{1,0:T(1,128)} %bitcast.1, bf16[256,256]{1,0:T(8,128)(2,1)} %constant.4.clone.fwd_hbm, ...), custom_call_target="tpu_custom_call" | custom-call | flops 4294967296 | bytes 8912896 | tf_op jit(solution)/shard_map/pallas_call | solution.py:479
  35.0 0.8 %copy.9 = bf16[1024,256]{1,0:T(8,128)(2,1)} copy(bf16[1024,256]{1,0:T(8,128)(2,1)S(1)} %shard_map.73) | data formatting | bytes 1048576

commit v4 on v3

--- a/solution.py
+++ b/solution.py
@@ -221,7 +221,7 @@
         return pl.ds(pl.multiple_of(start + j * piece_rows, piece_rows), piece_rows)
 
     def seam_first(j):
-        device = {"seq": seq_of(1, j, n_x - 1, n_core - 1)}
+        device = {"seq": seq_of(1, n_z - 1 - j, n_x - 1, n_core - 1)}
         return remote(xs.at[piece(j, rows)], relay, s_sem.at[j], r_sem.at[0], device)
 
     def seam_second(j):
@@ -316,6 +316,11 @@
     def _(i):
         gown[part(i)] = jnp.dot(feat[part(i)], wgt[3], preferred_element_type=jnp.float32)
 
+    @pl.when(relays & (z >= late))
+    def _():
+        seam_first(n_z - 1 - z).wait_recv()
+        seam_second(n_z - 1 - z).start()
+
     arrived(chunks - 2)
     g_copy(0).start()
 
@@ -328,11 +333,6 @@
 
     for i in range(1, chunks):
         g_copy(i).start()
-
-    @pl.when(relays)
-    def _():
-        seam_first(z).wait_recv()
-        seam_second(z).start()
 
     def forward(m):
         pair = xs[pl.ds(pl.multiple_of(m * block, block), 2 * block)]
@@ -406,9 +406,22 @@
         x_copy(d, (x + n_x - d) % n_x).wait_recv()
     c_copy(core).start()
 
+    @pl.when(relays & (z < late))
+    def _():
+        seam_first(n_z - 1 - z).wait_recv()
+        seam_second(n_z - 1 - z).start()
+
     @pl.when(me == 0)
     def _():
         xs[pl.ds(0, rows)] = jnp.zeros((rows, channels), xs.dtype)
+
+    def gate_of(i):
+        g_copy(i).wait_recv()
+        gate = gown[part(i)] + grecv[part(i)].astype(jnp.float32)
+        return gate / (1.0 + jnp.exp(-gate))
+
+    def gate_factor(i):
+        gown[part(i)] = gate_of(i)
 
     taps_last = (z < late) & (me != target)
 
@@ -422,6 +435,11 @@
     def _():
         transform_taps()
         products(blocks, 2 * blocks - 1)
+
+        @pl.when(me == target)
+        def _():
+            pl.loop(0, chunks)(gate_factor)
+
         transform_halo()
 
     products(0, blocks)
@@ -435,11 +453,17 @@
         direct = xs[pl.ds(pl.multiple_of(rows + a * block, block), block)].astype(jnp.float32)
         conv[pl.ds(pl.multiple_of(a * block, block), block)] = back + gain * direct
 
-    @pl.loop(0, chunks)
-    def _(i):
-        g_copy(i).wait_recv()
-        gate = gown[part(i)] + grecv[part(i)].astype(jnp.float32)
-        out[part(i)] = (conv[part(i)] * (gate / (1.0 + jnp.exp(-gate)))).astype(out.dtype)
+    @pl.when(me == target)
+    def _():
+        @pl.loop(0, chunks)
+        def _(i):
+            out[part(i)] = (conv[part(i)] * gown[part(i)]).astype(out.dtype)
+
+    @pl.when(me != target)
+    def _():
+        @pl.loop(0, chunks)
+        def _(i):
+            out[part(i)] = (conv[part(i)] * gate_of(i)).astype(out.dtype)
 
     for i in range(chunks):
         v_copy(i).wait_send()
@@ -464,7 +488,7 @@
 
     @pl.when(relays)
     def _():
-        seam_second(z).wait_send()
+        seam_second(n_z - 1 - z).wait_send()
 
 
 def solution(mesh, grid=GRID, blocks=BLOCKS, chunks=CHUNKS):

time: 35.9 us -> 35.4 us (0.986)
  Pallas kernels: 35 us -> 34.5 us
    pallas_call x1, Pallas kernels: 35 us -> 34.5 us  [on_device(): pl.pallas_call(functools.partial(layer, grid, blocks, chunks), out_shape=...]
where the time goes in v4:
time: 35.4 us; the launch traced here: 35.3 us
  Pallas kernels  34.5 us (97%)
  local copies, waits for them, and re-layouts  0.8 us (2%)
    pallas_call x1, Pallas kernels, on_device(): pl.pallas_call(functools.partial(layer, grid, blocks, chunks), out_shape=...  34.5 us
    unnamed x1, local copies, waits for them, and re-layouts  0.8 us

profile of v4, /device:TPU:24, one launch (start us, length us, event | category | flops | bytes accessed | tf_op | source)
XLA Modules:
  0.0 35.3 jit_solution(3369050543318723804)
XLA Ops:
  0.0 34.5 %shard_map.73 = bf16[1024,256]{1,0:T(8,128)(2,1)S(1)} custom-call(bf16[1024,2048]{1,0:T(8,128)(2,1)} %feat_hbm.1, bf16[2048,512]{1,0:T(8,128)(2,1)} %vw_hbm.1, bf16[2048,512]{1,0:T(8,128)(2,1)} %gw_hbm.1, bf16[8,256]{1,0:T(8,128)(2,1)} %ker_hbm.1, f32[1,256]{1,0:T(1,128)} %bitcast.1, bf16[256,256]{1,0:T(8,128)(2,1)} %constant.4.clone.fwd_hbm, ...), custom_call_target="tpu_custom_call" | custom-call | flops 4294967296 | bytes 8912896 | tf_op jit(solution)/shard_map/pallas_call | solution.py:503
  34.5 0.8 %copy.9 = bf16[1024,256]{1,0:T(8,128)(2,1)} copy(bf16[1024,256]{1,0:T(8,128)(2,1)S(1)} %shard_map.73) | data formatting | bytes 1048576

commit v5 on v4

--- a/solution.py
+++ b/solution.py
@@ -137,6 +137,7 @@
     source, target = n_seq // 2 - 1, n_seq // 2
     at_end = (x == n_x - 1) & (core == n_core - 1)
     is_source = me == source
+    direct = n_z // 2
     relays = at_end & (yh == 1)
     piece_rows = rows // n_z
     sends_halo = (me < n_seq - 1) & (me != source)
@@ -173,7 +174,7 @@
         for j in range(n_z):
             signal({"seq": seq_of(1, j, n_x - 1, n_core - 1)})
 
-    signal_if(relays, {"seq": source})
+    signal_if(relays | (me == target), {"seq": source})
 
     def count(*conditions):
         return sum(condition.astype(jnp.int32) for condition in conditions)
@@ -184,7 +185,7 @@
             level_count
             + jnp.where(z < late, z, n_z - 1)
             + count(leads, relays)
-            + jnp.where(is_source, n_z, 0),
+            + jnp.where(is_source, n_z + 1, 0),
         )
         for device, later, earlier in zip(z_devices, is_later, is_earlier):
             signal_if(later | earlier, device)
@@ -220,6 +221,11 @@
     def piece(j, start):
         return pl.ds(pl.multiple_of(start + j * piece_rows, piece_rows), piece_rows)
 
+    def seam_direct(j):
+        return remote(
+            xs.at[piece(j, rows)], xs.at[piece(j, 0)], s_sem.at[j], d_sem.at[j], {"seq": target}
+        )
+
     def seam_first(j):
         device = {"seq": seq_of(1, n_z - 1 - j, n_x - 1, n_core - 1)}
         return remote(xs.at[piece(j, rows)], relay, s_sem.at[j], r_sem.at[0], device)
@@ -275,7 +281,7 @@
         @pl.when(is_source)
         def _():
             for j in range(i * n_z // chunks, (i + 1) * n_z // chunks):
-                seam_first(j).start()
+                (seam_first(j) if j < direct else seam_direct(j)).start()
 
     a_copy(1 - yh).wait_recv()
 
@@ -316,7 +322,7 @@
     def _(i):
         gown[part(i)] = jnp.dot(feat[part(i)], wgt[3], preferred_element_type=jnp.float32)
 
-    @pl.when(relays & (z >= late))
+    @pl.when(relays & (z >= late) & (n_z - 1 - z < direct))
     def _():
         seam_first(n_z - 1 - z).wait_recv()
         seam_second(n_z - 1 - z).start()
@@ -392,7 +398,7 @@
             @pl.when(me == target)
             def _():
                 for j in range(i * n_z // chunks, (i + 1) * n_z // chunks):
-                    seam_second(j).wait_recv()
+                    (seam_second(j) if j < direct else seam_direct(j)).wait_recv()
 
             ready = blocks if i == chunks - 1 else (i + 1) * blocks // chunks - 1
             pl.loop(done, ready)(forward)
@@ -406,7 +412,7 @@
         x_copy(d, (x + n_x - d) % n_x).wait_recv()
     c_copy(core).start()
 
-    @pl.when(relays & (z < late))
+    @pl.when(relays & (z < late) & (n_z - 1 - z < direct))
     def _():
         seam_first(n_z - 1 - z).wait_recv()
         seam_second(n_z - 1 - z).start()
@@ -484,9 +490,9 @@
     @pl.when(is_source)
     def _():
         for j in range(n_z):
-            seam_first(j).wait_send()
-
-    @pl.when(relays)
+            (seam_first(j) if j < direct else seam_direct(j)).wait_send()
+
+    @pl.when(relays & (n_z - 1 - z < direct))
     def _():
         seam_second(n_z - 1 - z).wait_send()
 

time: 35.4 us -> 34 us (0.960)
  Pallas kernels: 34.5 us -> 32.9 us
    pallas_call x1, Pallas kernels: 34.5 us -> 32.9 us  [on_device(): pl.pallas_call(functools.partial(layer, grid, blocks, chunks), out_shape=...]
where the time goes in v5:
time: 34 us; the launch traced here: 33.7 us
  Pallas kernels  32.9 us (97%)
  local copies, waits for them, and re-layouts  0.8 us (2%)
    pallas_call x1, Pallas kernels, on_device(): pl.pallas_call(functools.partial(layer, grid, blocks, chunks), out_shape=...  32.9 us
    unnamed x1, local copies, waits for them, and re-layouts  0.8 us

profile of v5, /device:TPU:24, one launch (start us, length us, event | category | flops | bytes accessed | tf_op | source)
XLA Modules:
  0.0 33.7 jit_solution(11193633420666772229)
XLA Ops:
  0.0 32.9 %shard_map.73 = bf16[1024,256]{1,0:T(8,128)(2,1)S(1)} custom-call(bf16[1024,2048]{1,0:T(8,128)(2,1)} %feat_hbm.1, bf16[2048,512]{1,0:T(8,128)(2,1)} %vw_hbm.1, bf16[2048,512]{1,0:T(8,128)(2,1)} %gw_hbm.1, bf16[8,256]{1,0:T(8,128)(2,1)} %ker_hbm.1, f32[1,256]{1,0:T(1,128)} %bitcast.1, bf16[256,256]{1,0:T(8,128)(2,1)} %constant.4.clone.fwd_hbm, ...), custom_call_target="tpu_custom_call" | custom-call | flops 4294967296 | bytes 8912896 | tf_op jit(solution)/shard_map/pallas_call | solution.py:509
  32.9 0.8 %copy.9 = bf16[1024,256]{1,0:T(8,128)(2,1)} copy(bf16[1024,256]{1,0:T(8,128)(2,1)S(1)} %shard_map.73) | data formatting | bytes 1048576

commit v6 on v5

--- a/solution.py
+++ b/solution.py
@@ -307,14 +307,14 @@
         total = jnp.dot(feat[part(i)], wgt[2], preferred_element_type=jnp.float32)
         gsend[part(i)] = total.astype(gsend.dtype)
 
-    for i in range(early // 2, early):
-        arrived(i)
-
     @pl.when(z < late)
     def _():
         hear_answers()
         for d in range(1, n_z):
             z_copy(d, z).start()
+
+    for i in range(early // 2, early):
+        arrived(i)
 
     weight_copies[3].wait()
 

time: 34 us -> 33.8 us (level)
  no operation moved by 1% of the time
where the time goes in v6:
time: 33.8 us; the launch traced here: 33.7 us
  Pallas kernels  32.9 us (97%)
  local copies, waits for them, and re-layouts  0.8 us (2%)
    pallas_call x1, Pallas kernels, on_device(): pl.pallas_call(functools.partial(layer, grid, blocks, chunks), out_shape=...  32.9 us
    unnamed x1, local copies, waits for them, and re-layouts  0.8 us

profile of v6, /device:TPU:24, one launch (start us, length us, event | category | flops | bytes accessed | tf_op | source)
XLA Modules:
  0.0 33.7 jit_solution(13756899116344888305)
XLA Ops:
  0.0 32.9 %shard_map.73 = bf16[1024,256]{1,0:T(8,128)(2,1)S(1)} custom-call(bf16[1024,2048]{1,0:T(8,128)(2,1)} %feat_hbm.1, bf16[2048,512]{1,0:T(8,128)(2,1)} %vw_hbm.1, bf16[2048,512]{1,0:T(8,128)(2,1)} %gw_hbm.1, bf16[8,256]{1,0:T(8,128)(2,1)} %ker_hbm.1, f32[1,256]{1,0:T(1,128)} %bitcast.1, bf16[256,256]{1,0:T(8,128)(2,1)} %constant.4.clone.fwd_hbm, ...), custom_call_target="tpu_custom_call" | custom-call | flops 4294967296 | bytes 8912896 | tf_op jit(solution)/shard_map/pallas_call | solution.py:509
  32.9 0.8 %copy.9 = bf16[1024,256]{1,0:T(8,128)(2,1)} copy(bf16[1024,256]{1,0:T(8,128)(2,1)S(1)} %shard_map.73) | data formatting | bytes 1048576
